TPU v7x, 32 devices: a whole 2x2x4 slice. The times are simulated.
32 devices in a mesh: state: 4 (over y, core), aux: 2 (over x), cond: 4 (over z).
Axes of the slice: x: 2, y: 2, z: 4, core: 2. Of those that a mesh axis runs over, the one named last changes fastest.
Arguments:
- cond_pairs: float32 [8, 1024, 1024], P('aux', 'cond', 'state'), may hold values from -0.1875 to 0.1875
- val_pairs: float32 [8, 512, 512], P('aux', 'state', 'cond'), may hold values from -0.25 to 0.25
- screened: float32 [8, 8], replicated, may hold values from -0.75 to 0.75
- trials: float32 [8, 1024, 512], P('state', 'cond'), may hold values from -6 to 6
Outputs:
- response: float32 [8, 1024, 512], P('state', 'cond')
All inputs are finite; a program needn't handle non-finite values.
Results may differ from a plain program's by a relative error of at most 0.0001.
Values sent between devices are 32-bit elements; how exact they have to be, the bound alone decides.
A program may use at most 64 MiB of HBM per device.

v0:
```python
import functools

import jax
import jax.numpy as jnp
from jax import lax
from jax.experimental import pallas as pl
from jax.experimental.pallas import tpu as pltpu
from jax.sharding import PartitionSpec as P

highest = lax.Precision.HIGHEST
MESH = pl.DeviceIdType.MESH
UP, DOWN = 0, 1


def split(value):
    high = value.astype(jnp.bfloat16)
    low = (value - high.astype(jnp.float32)).astype(jnp.bfloat16)
    return high, low


def dot3(a_high, a_low, b_high, b_low):
    dot = functools.partial(jnp.dot, preferred_element_type=jnp.float32)
    return dot(a_high, b_high) + dot(a_high, b_low) + dot(a_low, b_high)


def kernel(
    n_cond,
    screened,
    b_own,
    v_own,
    x_own,
    out,
    v_got,
    b_raw,
    b_high,
    b_low,
    x_raw,
    c_raw,
    c_high,
    c_low,
    mixed,
    y_part,
    y_got,
    v_sems,
    b_sems,
    xz_sems,
    xx_sems,
    cz_sems,
    cy_sems,
    ck_sems,
    cf_sems,
    y_sems,
):
    s = lax.axis_index("state")
    a = lax.axis_index("aux")
    z = lax.axis_index("cond")
    aux_dev, rows, depth = b_own.shape
    n_trials = x_own.shape[0]
    half = rows // 2
    blk_v, blk_w = v_own.shape[1], v_own.shape[2]
    core_s = s + 1 - 2 * lax.rem(s, 2)
    y_s = lax.rem(s + 2, 4)
    far_s = lax.rem(core_s + 2, 4)
    x_mate = {"aux": 1 - a}
    y_mate = {"state": y_s}
    core_mate = {"state": core_s}
    z_next = ({"cond": z + 1}, {"cond": z - 1})
    has_next = (z + 1 < n_cond, z > 0)

    barrier = pltpu.get_barrier_semaphore()
    for mate in (x_mate, y_mate, core_mate):
        pl.semaphore_signal(barrier, inc=1, device_id=mate, device_id_type=MESH)
    for way in (UP, DOWN):

        @pl.when(has_next[way])
        def _():
            pl.semaphore_signal(barrier, inc=1, device_id=z_next[way], device_id_type=MESH)

    pl.semaphore_wait(
        barrier, 3 + has_next[UP].astype(jnp.int32) + has_next[DOWN].astype(jnp.int32)
    )

    sent = []

    def copy(src, dst, sems, index, mate):
        return pltpu.make_async_remote_copy(
            src_ref=src,
            dst_ref=dst,
            send_sem=sems.at[(0, *index)],
            recv_sem=sems.at[(1, *index)],
            device_id=mate,
            device_id_type=MESH,
        )

    def send(src, dst, sems, index, mate, where=None):
        if where is None:
            copy(src, dst, sems, index, mate).start()
        else:

            @pl.when(where)
            def _():
                copy(src, dst, sems, index, mate).start()

        sent.append((src, dst, sems, index, mate, where))

    def wait(dst, sems, index, mate):
        copy(dst, dst, sems, index, mate).wait_recv()

    def arrives(way, step):
        return z - step >= 0 if way == UP else z + step < n_cond

    def origin(way, step):
        return z - step if way == UP else z + step

    def x_slot(n, block, side):
        return x_raw.at[n, block, pl.ds(side * half, half)]

    def send_x_own(n):
        for way in (UP, DOWN):
            send(
                x_own.at[n, pl.ds(a * half, half)],
                x_slot(n, z, a),
                xz_sems,
                (n, way, 1),
                z_next[way],
                has_next[way],
            )

    def pass_x(n, step):
        for way in (UP, DOWN):
            here = arrives(way, step)
            slot = x_slot(n, jnp.clip(origin(way, step), 0, n_cond - 1), a)

            @pl.when(here)
            def _():
                wait(slot, xz_sems, (n, way, step), z_next[way])

            if step + 1 < n_cond:
                send(
                    slot, slot, xz_sems, (n, way, step + 1), z_next[way],
                    jnp.logical_and(here, has_next[way]),
                )
            send(slot, slot, xx_sems, (n, way, step), x_mate, here)

    def c_slot(state, block):
        return c_raw.at[state, block]

    def pass_c(step):
        for way in (UP, DOWN):
            here = arrives(way, step)
            slot = c_slot(s, jnp.clip(origin(way, step), 0, n_cond - 1))

            @pl.when(here)
            def _():
                wait(slot, cz_sems, (way, step), z_next[way])

            if step + 1 < n_cond:
                send(
                    slot, slot, cz_sems, (way, step + 1), z_next[way],
                    jnp.logical_and(here, has_next[way]),
                )
            send(slot, slot, cy_sems, (way, step), y_mate, here)
            send(slot, slot, ck_sems, (way, step), core_mate, here)

    def split_b(state, source):
        for p in range(aux_dev):
            high, low = split(source[p])
            b_high[state, p] = high
            b_low[state, p] = low

    def mix(n, block, value, first=False):
        x_high, x_low = split(value)

        @pl.loop(0, aux_dev)
        def _(p):
            term = dot3(b_high[block, p], b_low[block, p], x_high, x_low)
            if first:
                mixed[n, p] = term
            else:
                mixed[n, p] += term

    def mix_step(n, step):
        for way in (UP, DOWN):
            here = arrives(way, step)
            block = jnp.clip(origin(way, step), 0, n_cond - 1)

            @pl.when(here)
            def _():
                wait(x_slot(n, block, 1 - a), xx_sems, (n, way, step), x_mate)
                mix(n, block, x_raw[n, block])

    def apply(n, first, size):
        def term(p):
            m_high, m_low = split(mixed[n, p, first : first + size])
            return dot3(m_high, m_low, c_high[p], c_low[p])

        y_part[n, first : first + size] = term(0)

        @pl.loop(1, aux_dev)
        def _(p):
            y_part[n, first : first + size] += term(p)

        send(
            y_part.at[n, pl.ds(first, size)],
            y_got.at[n, pl.ds(first, size)],
            y_sems,
            (n, first // half),
            x_mate,
        )

    send(v_own, v_got, v_sems, (0,), x_mate)
    send_x_own(0)
    send(b_own, b_raw.at[s], b_sems, (0,), y_mate)
    send(b_own, b_raw.at[s], b_sems, (1,), core_mate)
    split_b(s, b_own)

    wait(v_got, v_sems, (0,), x_mate)
    for p in range(aux_dev):
        row = a * aux_dev + p
        total = screened[row, a * aux_dev] * v_own[0]
        for q in range(1, aux_dev):
            total += screened[row, a * aux_dev + q] * v_own[q]
        for q in range(aux_dev):
            total += screened[row, (1 - a) * aux_dev + q] * v_got[q]
        c_raw[s, z, p] = total
    own = c_slot(s, z)
    for way in (UP, DOWN):
        send(own, own, cz_sems, (way, 1), z_next[way], has_next[way])
    send(own, own, cy_sems, (UP, 0), y_mate)
    send(own, own, ck_sems, (UP, 0), core_mate)

    for step in range(1, n_cond):
        pass_x(0, step)
        if step == 1:
            pass_c(1)
    for n in range(1, n_trials):
        send_x_own(n)
    wait(b_raw.at[core_s], b_sems, (1,), core_mate)
    split_b(core_s, b_raw.at[core_s])
    wait(b_raw.at[y_s], b_sems, (0,), y_mate)
    send(b_raw.at[y_s], b_raw.at[y_s], b_sems, (2,), core_mate)
    for step in range(2, n_cond):
        pass_c(step)
    split_b(y_s, b_raw.at[y_s])
    wait(b_raw.at[far_s], b_sems, (2,), core_mate)
    split_b(far_s, b_raw.at[far_s])
    mix(0, z, x_own[0], first=True)
    for n in range(1, n_trials):
        pass_x(n, 1)
    for step in range(1, n_cond):
        mix_step(0, step)

    def each_c(sems, action):
        action((UP, 0), z, None)
        for step in range(1, n_cond):
            for way in (UP, DOWN):
                block = jnp.clip(origin(way, step), 0, n_cond - 1)
                action((way, step), block, arrives(way, step))

    def under(where, run):
        if where is None:
            run()
        else:
            pl.when(where)(run)

    def from_y(index, block, where):
        slot = c_slot(y_s, block)
        under(where, lambda: wait(slot, cy_sems, index, y_mate))
        send(slot, slot, cf_sems, index, core_mate, where)

    each_c(cy_sems, from_y)
    for n in range(1, n_trials):
        for step in range(2, n_cond):
            pass_x(n, step)

    def from_core(index, block, where):
        under(where, lambda: wait(c_slot(core_s, block), ck_sems, index, core_mate))

    def from_far(index, block, where):
        under(where, lambda: wait(c_slot(far_s, block), cf_sems, index, core_mate))

    each_c(ck_sems, from_core)
    each_c(cf_sems, from_far)
    for state in range(c_raw.shape[0]):
        for block in range(n_cond):
            place = (
                slice(None),
                slice(state * blk_v, (state + 1) * blk_v),
                slice(block * blk_w, (block + 1) * blk_w),
            )
            high, low = split(c_raw[state, block])
            c_high[place] = high
            c_low[place] = low

    apply(0, 0, half)
    apply(0, half, half)
    for n in range(1, n_trials):
        mix(n, z, x_own[n], first=True)
        for step in range(1, n_cond):
            mix_step(n, step)
        apply(n, 0, half)
        apply(n, half, half)
    for n in range(n_trials):
        for part in range(2):
            place = pl.ds(part * half, half)
            wait(y_got.at[n, place], y_sems, (n, part), x_mate)
            out[n, part * half : (part + 1) * half] = (
                y_part[n, part * half : (part + 1) * half]
                + y_got[n, part * half : (part + 1) * half]
            )
    for src, dst, sems, index, mate, where in sent:
        under(where, lambda: copy(src, dst, sems, index, mate).wait_send())


def fused(n_state, n_cond, cond_pairs, val_pairs, screened, trials):
    aux_dev, rows, depth = cond_pairs.shape
    n_trials, _, width = trials.shape
    blk_v, blk_w = val_pairs.shape[1:]
    f32, bf16 = jnp.float32, jnp.bfloat16
    dma = pltpu.SemaphoreType.DMA
    vmem = pl.BlockSpec(memory_space=pltpu.VMEM)
    macs = aux_dev * n_trials * rows * width * (n_state * depth + width)
    return pl.pallas_call(
        functools.partial(kernel, n_cond),
        out_shape=jax.ShapeDtypeStruct(trials.shape, f32),
        in_specs=[pl.BlockSpec(memory_space=pltpu.SMEM), vmem, vmem, vmem],
        out_specs=vmem,
        scratch_shapes=[
            pltpu.VMEM(val_pairs.shape, f32),
            pltpu.VMEM((n_state, *cond_pairs.shape), f32),
            pltpu.VMEM((n_state, *cond_pairs.shape), bf16),
            pltpu.VMEM((n_state, *cond_pairs.shape), bf16),
            pltpu.VMEM((n_trials, n_cond, rows, width), f32),
            pltpu.VMEM((n_state, n_cond, *val_pairs.shape), f32),
            pltpu.VMEM((aux_dev, width, width), bf16),
            pltpu.VMEM((aux_dev, width, width), bf16),
            pltpu.VMEM((n_trials, aux_dev, rows, width), f32),
            pltpu.VMEM(trials.shape, f32),
            pltpu.VMEM(trials.shape, f32),
            dma((2, 1)),
            dma((2, 3)),
            dma((2, n_trials, 2, n_cond)),
            dma((2, n_trials, 2, n_cond)),
            dma((2, 2, n_cond)),
            dma((2, 2, n_cond)),
            dma((2, 2, n_cond)),
            dma((2, 2, n_cond)),
            dma((2, n_trials, 2)),
        ],
        compiler_params=pltpu.CompilerParams(
            collective_id=0, has_side_effects=True, vmem_limit_bytes=56 * 1024 * 1024
        ),
        cost_estimate=pl.CostEstimate(
            flops=6 * macs, bytes_accessed=4 * (2 * trials.size + cond_pairs.size), transcendentals=0
        ),
    )(screened, cond_pairs, val_pairs, trials)


def gathered(cond_pairs, val_pairs, screened, trials):
    aux_dev = cond_pairs.shape[0]
    aux_first = lax.axis_index("aux") * aux_dev
    own_rows = lax.dynamic_slice_in_dim(screened, aux_first, aux_dev, 0)
    coupled = jnp.einsum(
        "pq,qab->pab",
        own_rows,
        lax.all_gather(val_pairs, "aux", axis=0, tiled=True),
        precision=highest,
    )
    n_state = lax.axis_size("state")
    n_cond = lax.axis_size("cond")
    rows_state = coupled.shape[1]
    cols_cond = coupled.shape[2]
    pieces = lax.all_gather(coupled[None], ("state", "cond"), axis=0, tiled=True)
    coupled_full = pieces.reshape(n_state, n_cond, aux_dev, rows_state, cols_cond)
    coupled_full = coupled_full.transpose(2, 0, 3, 1, 4).reshape(
        aux_dev, n_state * rows_state, n_cond * cols_cond
    )
    everything = lax.all_gather(trials, "cond", axis=1, tiled=True)
    mixture = jnp.einsum(
        "pcd,ndv->pncv",
        lax.all_gather(cond_pairs, "state", axis=2, tiled=True),
        everything,
        precision=highest,
    )
    partial_value = jnp.einsum("pncv,pvw->ncw", mixture, coupled_full, precision=highest)
    return lax.psum(partial_value, "aux")


def solution(mesh):
    n_state, n_cond = mesh.shape["state"], mesh.shape["cond"]
    in_specs = (P("aux", "cond", "state"), P("aux", "state", "cond"), P(), P("state", "cond", None))
    out_specs = P("state", "cond", None)
    if mesh.shape["aux"] == 2 and n_state == 4 and n_cond == n_state:
        per_device = functools.partial(fused, n_state, n_cond)
    else:
        per_device = gathered
    return jax.shard_map(
        per_device, mesh=mesh, in_specs=in_specs, out_specs=out_specs, check_vma=False
    )
```

profile of v0, /device:TPU:0, one launch (start us, length us, event | category | flops | bytes accessed | tf_op | source)
XLA Modules:
  0.0 94.4 jit_solution(16509264909712682185)
XLA Ops:
  0.0 92.1 %shard_map.46 = f32[2,256,512]{2,1,0:T(8,128)} custom-call(f32[8,8]{1,0:T(8,128)} %screened.1, f32[4,256,256]{2,1,0:T(8,128)} %b_own.1, f32[4,128,128]{2,1,0:T(8,128)} %v_own.1, f32[2,256,512]{2,1,0:T(8,128)} %x_own.1), custom_call_target="tpu_custom_call" | custom-call | flops 9663676416 | bytes 3145728 | tf_op jit(solution)/shard_map/pallas_call | solution.py:323
  92.2 2.3 %copy.6 = f32[2,256,512]{2,1,0:T(8,128)} copy(f32[2,256,512]{2,1,0:T(8,128)} %shard_map.46) | data formatting | bytes 2097152
where the time goes:
time: 94.6 us; the launch traced here: 94.4 us
  Pallas kernels  92.1 us (97%)
  local copies, waits for them, and re-layouts  2.26 us (2%)
    pallas_call x1, Pallas kernels, fused(): pl.pallas_call(functools.partial(kernel, n_cond), out_shape=jax.ShapeDtyp...  92.1 us
    unnamed x1, local copies, waits for them, and re-layouts  2.26 us

commit v1 on v0

--- a/solution.py
+++ b/solution.py
@@ -36,9 +36,9 @@
     b_low,
     x_raw,
     c_raw,
-    c_high,
-    c_low,
     mixed,
+    m_high,
+    m_low,
     y_part,
     y_got,
     v_sems,
@@ -179,37 +179,54 @@
             else:
                 mixed[n, p] += term
 
-    def mix_step(n, step):
+    def mix_step(step):
         for way in (UP, DOWN):
             here = arrives(way, step)
             block = jnp.clip(origin(way, step), 0, n_cond - 1)
 
             @pl.when(here)
             def _():
-                wait(x_slot(n, block, 1 - a), xx_sems, (n, way, step), x_mate)
-                mix(n, block, x_raw[n, block])
-
-    def apply(n, first, size):
-        def term(p):
-            m_high, m_low = split(mixed[n, p, first : first + size])
-            return dot3(m_high, m_low, c_high[p], c_low[p])
-
-        y_part[n, first : first + size] = term(0)
-
-        @pl.loop(1, aux_dev)
+                for n in range(n_trials):
+                    wait(x_slot(n, block, 1 - a), xx_sems, (n, way, step), x_mate)
+                    mix(n, block, x_raw[n, block])
+
+    def from_y(index, block):
+        slot = c_slot(y_s, block)
+        wait(slot, cy_sems, index, y_mate)
+        copy(slot, slot, cf_sems, index, core_mate).start()
+
+    def apply(index, block):
+        wait(c_slot(core_s, block), ck_sems, index, core_mate)
+        wait(c_slot(far_s, block), cf_sems, index, core_mate)
+
+        @pl.loop(0, aux_dev)
         def _(p):
-            y_part[n, first : first + size] += term(p)
-
-        send(
-            y_part.at[n, pl.ds(first, size)],
-            y_got.at[n, pl.ds(first, size)],
-            y_sems,
-            (n, first // half),
-            x_mate,
-        )
+            c_high, c_low = split(c_raw[:, block, p].reshape(-1, blk_w))
+            for n in range(n_trials):
+                term = dot3(m_high[n, p], m_low[n, p], c_high, c_low)
+                prior = y_part[block, n]
+                y_part[block, n] = jnp.where(p == 0, term, prior + term)
+
+        copy(y_part.at[block], y_got.at[block], y_sems, index, x_mate).start()
+
+    def finish(index, block):
+        wait(y_got.at[block], y_sems, index, x_mate)
+        columns = pl.ds(pl.multiple_of(block * blk_w, blk_w), blk_w)
+        for n in range(n_trials):
+            out[n, :, columns] = y_part[block, n] + y_got[block, n]
+
+    def at_step(step, *actions):
+        for way in (UP, DOWN):
+            block = jnp.clip(origin(way, step), 0, n_cond - 1)
+
+            @pl.when(arrives(way, step))
+            def _():
+                for action in actions:
+                    action((way, step), block)
 
     send(v_own, v_got, v_sems, (0,), x_mate)
-    send_x_own(0)
+    for n in range(n_trials):
+        send_x_own(n)
     send(b_own, b_raw.at[s], b_sems, (0,), y_mate)
     send(b_own, b_raw.at[s], b_sems, (1,), core_mate)
     split_b(s, b_own)
@@ -224,38 +241,58 @@
             total += screened[row, (1 - a) * aux_dev + q] * v_got[q]
         c_raw[s, z, p] = total
     own = c_slot(s, z)
+    own_index = (UP, 0)
+    send(own, own, cy_sems, own_index, y_mate)
+    send(own, own, ck_sems, own_index, core_mate)
+
+    def pass_all(step):
+        for n in range(n_trials):
+            pass_x(n, step)
+
+    for step in range(1, n_cond - 1):
+        pass_all(step)
     for way in (UP, DOWN):
         send(own, own, cz_sems, (way, 1), z_next[way], has_next[way])
-    send(own, own, cy_sems, (UP, 0), y_mate)
-    send(own, own, ck_sems, (UP, 0), core_mate)
-
-    for step in range(1, n_cond):
-        pass_x(0, step)
-        if step == 1:
-            pass_c(1)
-    for n in range(1, n_trials):
-        send_x_own(n)
+    wait(b_raw.at[y_s], b_sems, (0,), y_mate)
+    send(b_raw.at[y_s], b_raw.at[y_s], b_sems, (2,), core_mate)
     wait(b_raw.at[core_s], b_sems, (1,), core_mate)
     split_b(core_s, b_raw.at[core_s])
-    wait(b_raw.at[y_s], b_sems, (0,), y_mate)
-    send(b_raw.at[y_s], b_raw.at[y_s], b_sems, (2,), core_mate)
-    for step in range(2, n_cond):
-        pass_c(step)
     split_b(y_s, b_raw.at[y_s])
     wait(b_raw.at[far_s], b_sems, (2,), core_mate)
     split_b(far_s, b_raw.at[far_s])
-    mix(0, z, x_own[0], first=True)
-    for n in range(1, n_trials):
-        pass_x(n, 1)
+    from_y(own_index, z)
+    for n in range(n_trials):
+        mix(n, z, x_own[n], first=True)
+    mix_step(1)
+    pass_all(n_cond - 1)
+    pass_c(1)
+    for step in range(2, n_cond):
+        mix_step(step)
+
+    @pl.loop(0, aux_dev)
+    def _(p):
+        for n in range(n_trials):
+            high, low = split(mixed[n, p])
+            m_high[n, p] = high
+            m_low[n, p] = low
+
+    apply(own_index, z)
     for step in range(1, n_cond):
-        mix_step(0, step)
-
-    def each_c(sems, action):
-        action((UP, 0), z, None)
-        for step in range(1, n_cond):
-            for way in (UP, DOWN):
-                block = jnp.clip(origin(way, step), 0, n_cond - 1)
-                action((way, step), block, arrives(way, step))
+        at_step(step, from_y)
+        if step + 1 < n_cond:
+            pass_c(step + 1)
+        at_step(step, apply)
+    finish(own_index, z)
+    for step in range(1, n_cond):
+        at_step(step, finish)
+
+    def sent_out(index, block):
+        copy(c_slot(y_s, block), c_slot(y_s, block), cf_sems, index, core_mate).wait_send()
+        copy(y_part.at[block], y_got.at[block], y_sems, index, x_mate).wait_send()
+
+    sent_out(own_index, z)
+    for step in range(1, n_cond):
+        at_step(step, sent_out)
 
     def under(where, run):
         if where is None:
@@ -263,51 +300,6 @@
         else:
             pl.when(where)(run)
 
-    def from_y(index, block, where):
-        slot = c_slot(y_s, block)
-        under(where, lambda: wait(slot, cy_sems, index, y_mate))
-        send(slot, slot, cf_sems, index, core_mate, where)
-
-    each_c(cy_sems, from_y)
-    for n in range(1, n_trials):
-        for step in range(2, n_cond):
-            pass_x(n, step)
-
-    def from_core(index, block, where):
-        under(where, lambda: wait(c_slot(core_s, block), ck_sems, index, core_mate))
-
-    def from_far(index, block, where):
-        under(where, lambda: wait(c_slot(far_s, block), cf_sems, index, core_mate))
-
-    each_c(ck_sems, from_core)
-    each_c(cf_sems, from_far)
-    for state in range(c_raw.shape[0]):
-        for block in range(n_cond):
-            place = (
-                slice(None),
-                slice(state * blk_v, (state + 1) * blk_v),
-                slice(block * blk_w, (block + 1) * blk_w),
-            )
-            high, low = split(c_raw[state, block])
-            c_high[place] = high
-            c_low[place] = low
-
-    apply(0, 0, half)
-    apply(0, half, half)
-    for n in range(1, n_trials):
-        mix(n, z, x_own[n], first=True)
-        for step in range(1, n_cond):
-            mix_step(n, step)
-        apply(n, 0, half)
-        apply(n, half, half)
-    for n in range(n_trials):
-        for part in range(2):
-            place = pl.ds(part * half, half)
-            wait(y_got.at[n, place], y_sems, (n, part), x_mate)
-            out[n, part * half : (part + 1) * half] = (
-                y_part[n, part * half : (part + 1) * half]
-                + y_got[n, part * half : (part + 1) * half]
-            )
     for src, dst, sems, index, mate, where in sent:
         under(where, lambda: copy(src, dst, sems, index, mate).wait_send())
 
@@ -332,11 +324,11 @@
             pltpu.VMEM((n_state, *cond_pairs.shape), bf16),
             pltpu.VMEM((n_trials, n_cond, rows, width), f32),
             pltpu.VMEM((n_state, n_cond, *val_pairs.shape), f32),
-            pltpu.VMEM((aux_dev, width, width), bf16),
-            pltpu.VMEM((aux_dev, width, width), bf16),
             pltpu.VMEM((n_trials, aux_dev, rows, width), f32),
-            pltpu.VMEM(trials.shape, f32),
-            pltpu.VMEM(trials.shape, f32),
+            pltpu.VMEM((n_trials, aux_dev, rows, width), bf16),
+            pltpu.VMEM((n_trials, aux_dev, rows, width), bf16),
+            pltpu.VMEM((n_cond, n_trials, rows, blk_w), f32),
+            pltpu.VMEM((n_cond, n_trials, rows, blk_w), f32),
             dma((2, 1)),
             dma((2, 3)),
             dma((2, n_trials, 2, n_cond)),
@@ -345,7 +337,7 @@
             dma((2, 2, n_cond)),
             dma((2, 2, n_cond)),
             dma((2, 2, n_cond)),
-            dma((2, n_trials, 2)),
+            dma((2, 2, n_cond)),
         ],
         compiler_params=pltpu.CompilerParams(
             collective_id=0, has_side_effects=True, vmem_limit_bytes=56 * 1024 * 1024

time: 94.6 us -> 85 us (0.90)
  Pallas kernels: 92.1 us -> 82.6 us
    pallas_call x1, Pallas kernels: 92.1 us -> 82.6 us  [fused(): pl.pallas_call(functools.partial(kernel, n_cond), out_shape=jax.ShapeDtyp...]
where the time goes in v1:
time: 85 us; the launch traced here: 84.9 us
  Pallas kernels  82.6 us (97%)
  local copies, waits for them, and re-layouts  2.26 us (3%)
    pallas_call x1, Pallas kernels, fused(): pl.pallas_call(functools.partial(kernel, n_cond), out_shape=jax.ShapeDtyp...  82.6 us
    unnamed x1, local copies, waits for them, and re-layouts  2.26 us

profile of v1, /device:TPU:0, one launch (start us, length us, event | category | flops | bytes accessed | tf_op | source)
XLA Modules:
  0.0 84.9 jit_solution(15408093589118961806)
XLA Ops:
  0.0 82.6 %shard_map.46 = f32[2,256,512]{2,1,0:T(8,128)} custom-call(f32[8,8]{1,0:T(8,128)} %screened.1, f32[4,256,256]{2,1,0:T(8,128)} %b_own.1, f32[4,128,128]{2,1,0:T(8,128)} %v_own.1, f32[2,256,512]{2,1,0:T(8,128)} %x_own.1), custom_call_target="tpu_custom_call" | custom-call | flops 9663676416 | bytes 3145728 | tf_op jit(solution)/shard_map/pallas_call | solution.py:315
  82.6 2.3 %copy.6 = f32[2,256,512]{2,1,0:T(8,128)} copy(f32[2,256,512]{2,1,0:T(8,128)} %shard_map.46) | data formatting | bytes 2097152

commit v2 on v1

--- a/solution.py
+++ b/solution.py
@@ -50,6 +50,7 @@
     ck_sems,
     cf_sems,
     y_sems,
+    yo_sems,
 ):
     s = lax.axis_index("state")
     a = lax.axis_index("aux")
@@ -171,7 +172,7 @@
     def mix(n, block, value, first=False):
         x_high, x_low = split(value)
 
-        @pl.loop(0, aux_dev)
+        @pl.loop(0, aux_dev, unroll=2)
         def _(p):
             term = dot3(b_high[block, p], b_low[block, p], x_high, x_low)
             if first:
@@ -179,38 +180,56 @@
             else:
                 mixed[n, p] += term
 
-    def mix_step(step):
+    def mix_step(n, step):
         for way in (UP, DOWN):
             here = arrives(way, step)
             block = jnp.clip(origin(way, step), 0, n_cond - 1)
 
             @pl.when(here)
             def _():
-                for n in range(n_trials):
-                    wait(x_slot(n, block, 1 - a), xx_sems, (n, way, step), x_mate)
-                    mix(n, block, x_raw[n, block])
+                wait(x_slot(n, block, 1 - a), xx_sems, (n, way, step), x_mate)
+                mix(n, block, x_raw[n, block])
+
+    def split_m(n):
+        @pl.loop(0, aux_dev)
+        def _(p):
+            high, low = split(mixed[n, p])
+            m_high[n, p] = high
+            m_low[n, p] = low
 
     def from_y(index, block):
         slot = c_slot(y_s, block)
         wait(slot, cy_sems, index, y_mate)
         copy(slot, slot, cf_sems, index, core_mate).start()
 
-    def apply(index, block):
-        wait(c_slot(core_s, block), ck_sems, index, core_mate)
-        wait(c_slot(far_s, block), cf_sems, index, core_mate)
-
-        @pl.loop(0, aux_dev)
+    def respond(ns, block):
+        @pl.loop(0, aux_dev, unroll=2)
         def _(p):
             c_high, c_low = split(c_raw[:, block, p].reshape(-1, blk_w))
-            for n in range(n_trials):
+            for n in ns:
                 term = dot3(m_high[n, p], m_low[n, p], c_high, c_low)
                 prior = y_part[block, n]
                 y_part[block, n] = jnp.where(p == 0, term, prior + term)
 
+    def wait_c(index, block):
+        wait(c_slot(core_s, block), ck_sems, index, core_mate)
+        wait(c_slot(far_s, block), cf_sems, index, core_mate)
+
+    def apply(index, block):
+        wait_c(index, block)
+        respond(range(n_trials), block)
         copy(y_part.at[block], y_got.at[block], y_sems, index, x_mate).start()
 
+    def apply_own(n):
+        respond([n], z)
+        send(y_part.at[z, n], y_got.at[z, n], yo_sems, (n,), x_mate)
+
     def finish(index, block):
-        wait(y_got.at[block], y_sems, index, x_mate)
+        if index == own_index:
+            for n in range(n_trials):
+                wait(y_got.at[block, n], yo_sems, (n,), x_mate)
+        else:
+            wait(y_got.at[block], y_sems, index, x_mate)
         columns = pl.ds(pl.multiple_of(block * blk_w, blk_w), blk_w)
         for n in range(n_trials):
             out[n, :, columns] = y_part[block, n] + y_got[block, n]
@@ -253,33 +272,33 @@
         pass_all(step)
     for way in (UP, DOWN):
         send(own, own, cz_sems, (way, 1), z_next[way], has_next[way])
+    wait(b_raw.at[core_s], b_sems, (1,), core_mate)
+    split_b(core_s, b_raw.at[core_s])
     wait(b_raw.at[y_s], b_sems, (0,), y_mate)
     send(b_raw.at[y_s], b_raw.at[y_s], b_sems, (2,), core_mate)
-    wait(b_raw.at[core_s], b_sems, (1,), core_mate)
-    split_b(core_s, b_raw.at[core_s])
     split_b(y_s, b_raw.at[y_s])
     wait(b_raw.at[far_s], b_sems, (2,), core_mate)
     split_b(far_s, b_raw.at[far_s])
     from_y(own_index, z)
     for n in range(n_trials):
         mix(n, z, x_own[n], first=True)
-    mix_step(1)
+        mix_step(n, 1)
     pass_all(n_cond - 1)
     pass_c(1)
-    for step in range(2, n_cond):
-        mix_step(step)
-
-    @pl.loop(0, aux_dev)
-    def _(p):
-        for n in range(n_trials):
-            high, low = split(mixed[n, p])
-            m_high[n, p] = high
-            m_low[n, p] = low
-
-    apply(own_index, z)
+    wait_c(own_index, z)
+    for n in range(n_trials):
+        for step in range(2, n_cond):
+            mix_step(n, step)
+        if n == n_trials - 1:
+            at_step(1, from_y)
+            pass_c(2)
+        split_m(n)
+        apply_own(n)
+
     for step in range(1, n_cond):
-        at_step(step, from_y)
-        if step + 1 < n_cond:
+        if step > 1:
+            at_step(step, from_y)
+        if 1 < step < n_cond - 1:
             pass_c(step + 1)
         at_step(step, apply)
     finish(own_index, z)
@@ -288,7 +307,8 @@
 
     def sent_out(index, block):
         copy(c_slot(y_s, block), c_slot(y_s, block), cf_sems, index, core_mate).wait_send()
-        copy(y_part.at[block], y_got.at[block], y_sems, index, x_mate).wait_send()
+        if index != own_index:
+            copy(y_part.at[block], y_got.at[block], y_sems, index, x_mate).wait_send()
 
     sent_out(own_index, z)
     for step in range(1, n_cond):
@@ -338,6 +358,7 @@
             dma((2, 2, n_cond)),
             dma((2, 2, n_cond)),
             dma((2, 2, n_cond)),
+            dma((2, n_trials)),
         ],
         compiler_params=pltpu.CompilerParams(
             collective_id=0, has_side_effects=True, vmem_limit_bytes=56 * 1024 * 1024

time: 85 us -> 80.9 us (0.952)
  Pallas kernels: 82.6 us -> 78.3 us
    pallas_call x1, Pallas kernels: 82.6 us -> 78.3 us  [fused(): pl.pallas_call(functools.partial(kernel, n_cond), out_shape=jax.ShapeDtyp...]
where the time goes in v2:
time: 80.9 us; the launch traced here: 80.6 us
  Pallas kernels  78.3 us (97%)
  local copies, waits for them, and re-layouts  2.26 us (3%)
    pallas_call x1, Pallas kernels, fused(): pl.pallas_call(functools.partial(kernel, n_cond), out_shape=jax.ShapeDtyp...  78.3 us
    unnamed x1, local copies, waits for them, and re-layouts  2.26 us

profile of v2, /device:TPU:0, one launch (start us, length us, event | category | flops | bytes accessed | tf_op | source)
XLA Modules:
  0.0 80.6 jit_solution(2082224704796636080)
XLA Ops:
  0.0 78.3 %shard_map.46 = f32[2,256,512]{2,1,0:T(8,128)} custom-call(f32[8,8]{1,0:T(8,128)} %screened.1, f32[4,256,256]{2,1,0:T(8,128)} %b_own.1, f32[4,128,128]{2,1,0:T(8,128)} %v_own.1, f32[2,256,512]{2,1,0:T(8,128)} %x_own.1), custom_call_target="tpu_custom_call" | custom-call | flops 9663676416 | bytes 3145728 | tf_op jit(solution)/shard_map/pallas_call | solution.py:335
  78.3 2.3 %copy.6 = f32[2,256,512]{2,1,0:T(8,128)} copy(f32[2,256,512]{2,1,0:T(8,128)} %shard_map.46) | data formatting | bytes 2097152
